TPU v7x, 32 devices: a whole 2x2x4 slice. The times are simulated.
32 devices in a mesh: slab: 2 (over y), blk: 4 (over z), bag: 2 (over x), sub: 2 (over core).
Axes of the slice: x: 2, y: 2, z: 4, core: 2. Of those that a mesh axis runs over, the one named last changes fastest.
Arguments:
- real_points: bfloat16 [64, 8192], P(None, ('slab', 'blk')), parts along dimension 1, may hold values from -4 to 4
- synth_points: bfloat16 [64, 8192], P(None, ('slab', 'blk')), parts along dimension 1, may hold values from -4 to 4
- real_cluster: int32 [8192], P(('slab', 'blk')), parts along dimension 0, may hold values from 0 to 3
- synth_cluster: int32 [8192], P(('slab', 'blk')), parts along dimension 0, may hold values from 0 to 3
- real_weight: int32 [32, 8192], P('bag', ('slab', 'blk')), parts along dimension 1, may hold values from 0 to 4
- synth_weight: int32 [32, 8192], P('bag', ('slab', 'blk')), parts along dimension 1, may hold values from 0 to 4
- pair_block: int32 [64, 2], P(('slab', 'blk', 'sub')), parts along dimension 0, may hold values from 0 to 7, as said below
- pair_row: int32 [64, 2], P(('slab', 'blk', 'sub')), parts along dimension 0, may hold values from 0 to 7
- pair_count: int32 [64], P(('slab', 'blk', 'sub')), parts along dimension 0, may hold values from 1 to 2, as said below
Outputs:
- real_potential: float32 [32, 8192], P('bag', ('slab', 'blk')), parts along dimension 1
- synth_potential: float32 [32, 8192], P('bag', ('slab', 'blk')), parts along dimension 1
There are 2 independent parts, one for each index of `slab`. A program takes and returns all parts, laid end to end along the dimension named above; each array names one. Nothing has to cross between parts.
Inputs may be any that keep to these rules, and one draw needn't show every extreme that they name: `pair_block`: row 4 * (2 * b + s) + p belongs to the device at blk index b and sub index s; all listed pairs of the whole list are distinct. `pair_count`: in every draw all devices of one sub index list 2 pairs with one blk index.
All inputs are finite; a program needn't handle non-finite values.
Results may differ from a plain program's by a relative error of at most 0.0015.
Values may be sent and summed in bfloat16 or wider, within the bound.
A program may use at most 64 MiB of HBM per device.

v0:
```python
import math

import jax
import jax.numpy as jnp
from jax import lax
from jax.sharding import PartitionSpec as P

BLOCK = 128
ITERS = 2


SMOOTH = 0.1
PENALTY = 0.3
SENTINEL = -1e30


def joined(value, axis, join):
    pieces = jax.tree.map(lambda part: lax.all_gather(part, axis), value)
    head = jax.tree.map(lambda part: part[0], pieces)
    tail = jax.tree.map(lambda part: part[1:], pieces)
    subtotal, _ = lax.scan(lambda subtotal, share: (join(subtotal, share), None), head, tail)
    return subtotal


def join_parts(earlier, latter):
    larger = jnp.maximum(earlier[0], latter[0])
    return (
        larger,
        earlier[1] * jnp.exp(earlier[0] - larger) + latter[1] * jnp.exp(latter[0] - larger),
    )


def fold_blocks(highest, mass_sum, owners, blocks):
    matches = owners[:, None] == jnp.arange(blocks, dtype=jnp.int32)[None, :]
    match_mask = matches[None, :, :, None]
    block_top = jnp.max(jnp.where(match_mask, highest[:, :, None, :], SENTINEL), axis=1)
    slot_top = jnp.take(block_top, owners, axis=1)
    scaled = mass_sum * jnp.exp(highest - slot_top)
    summed = jnp.sum(jnp.where(match_mask, scaled[:, :, None, :], 0.0), axis=1)
    return (block_top, summed)


def finish(log_weight, block_top, summed):
    spread = jnp.where(summed > 0.5, block_top + jnp.log(jnp.maximum(summed, 0.5)), 0.0)
    return SMOOTH * log_weight - SMOOTH * spread


def slot_costs(slot_real, slot_real_tag, slot_synth, slot_synth_tag):
    inner_prod = jnp.einsum(
        "dgi,dgj->gij", slot_real, slot_synth, preferred_element_type=jnp.float32
    )
    real_sq = jnp.sum(jnp.square(slot_real.astype(jnp.float32)), axis=0)
    synth_sq = jnp.sum(jnp.square(slot_synth.astype(jnp.float32)), axis=0)
    differ = (slot_real_tag[:, :, None] != slot_synth_tag[:, None, :]).astype(jnp.float32)
    return 0.5 * real_sq[:, :, None] + 0.5 * synth_sq[:, None, :] - inner_prod + PENALTY * differ


def sweep(slot_x, slot_tags, far_y, far_tags, panel_rows, along_rows, group_size):
    marginals, slot_count, width_pts = panel_rows.shape
    group_total = slot_count // group_size

    def one_group(group_index):
        first_slot = group_index * group_size
        pair_cost = slot_costs(
            lax.dynamic_slice_in_dim(slot_x, first_slot, group_size, 1),
            lax.dynamic_slice_in_dim(slot_tags, first_slot, group_size, 0),
            lax.dynamic_slice_in_dim(far_y, first_slot, group_size, 1),
            lax.dynamic_slice_in_dim(far_tags, first_slot, group_size, 0),
        )
        panel_part = lax.dynamic_slice_in_dim(panel_rows, first_slot, group_size, 1)
        if along_rows:
            scores = (panel_part[:, :, None, :] - pair_cost[None]) / SMOOTH
            highest = jnp.max(scores, axis=3)
            mass_sum = jnp.sum(jnp.exp(scores - highest[:, :, :, None]), axis=3)
        else:
            scores = (panel_part[:, :, :, None] - pair_cost[None]) / SMOOTH
            highest = jnp.max(scores, axis=2)
            mass_sum = jnp.sum(jnp.exp(scores - highest[:, :, None, :]), axis=2)
        return (highest, mass_sum)

    highest, mass_sum = lax.map(one_group, jnp.arange(group_total, dtype=jnp.int32))
    highest = jnp.transpose(highest, (1, 0, 2, 3)).reshape(marginals, slot_count, width_pts)
    mass_sum = jnp.transpose(mass_sum, (1, 0, 2, 3)).reshape(marginals, slot_count, width_pts)
    return (highest, mass_sum)


def fetch_panel(synth_pot, requested, global_col):
    marginals, blocks, width_pts = synth_pot.shape
    replies = jnp.take(synth_pot, requested, axis=1)
    arrived = lax.all_to_all(replies, "blk", split_axis=1, concat_axis=1, tiled=True)
    return arrived.reshape(marginals, global_col.shape[0], width_pts)


def column_update(highest, mass_sum, requested, log_synth):
    marginals, blocks, width_pts = log_synth.shape
    peer_count, capacity = requested.shape
    back_top, back_sum = (
        lax.all_to_all(
            highest.reshape(marginals, peer_count, capacity, width_pts),
            "blk",
            split_axis=1,
            concat_axis=1,
            tiled=True,
        ),
        lax.all_to_all(
            mass_sum.reshape(marginals, peer_count, capacity, width_pts),
            "blk",
            split_axis=1,
            concat_axis=1,
            tiled=True,
        ),
    )
    block_top, summed = fold_blocks(
        back_top.reshape(marginals, peer_count * capacity, width_pts),
        back_sum.reshape(marginals, peer_count * capacity, width_pts),
        requested.reshape(peer_count * capacity),
        blocks,
    )
    block_top, summed = joined((block_top, summed), "sub", join_parts)
    return finish(log_synth, block_top, summed)


def shards(
    real_points,
    synth_points,
    real_cluster,
    synth_cluster,
    real_weight,
    synth_weight,
    pair_block,
    pair_row,
    pair_count,
):
    features, point_count = real_points.shape
    blocks = point_count // BLOCK
    marginals = real_weight.shape[0]
    peer_count, capacity = pair_block.shape
    slot_count = peer_count * capacity
    group_size = math.gcd(slot_count, 4)
    own_real = real_points.reshape(features, blocks, BLOCK)
    own_synth = synth_points.reshape(features, blocks, BLOCK)
    real_tags = real_cluster.reshape(blocks, BLOCK).astype(jnp.bfloat16)
    synth_tags = synth_cluster.reshape(1, blocks, BLOCK).astype(jnp.bfloat16)
    log_real = jnp.log(real_weight.astype(jnp.float32) + 0.5).reshape(marginals, blocks, BLOCK)
    log_synth = jnp.log(synth_weight.astype(jnp.float32) + 0.5).reshape(marginals, blocks, BLOCK)
    listed = lax.broadcasted_iota(jnp.int32, (peer_count, capacity), 1) < pair_count[:, None]
    wanted = jnp.where(listed, pair_block, 0)
    rows_used = jnp.where(listed, pair_row, 0).reshape(slot_count)
    usable = listed.reshape(slot_count)[None, :, None]
    global_col = (jnp.arange(peer_count, dtype=jnp.int32)[:, None] * blocks + wanted).reshape(
        slot_count
    )
    requested = lax.all_to_all(wanted, "blk", split_axis=0, concat_axis=0, tiled=True)
    far_y, far_tags = (
        lax.all_to_all(
            jnp.take(own_synth, requested, axis=1), "blk", split_axis=1, concat_axis=1, tiled=True
        ),
        lax.all_to_all(
            jnp.take(synth_tags, requested, axis=1), "blk", split_axis=1, concat_axis=1, tiled=True
        ),
    )
    far_y = far_y.reshape(features, slot_count, BLOCK)
    far_tags = far_tags.reshape(slot_count, BLOCK)
    slot_x = jnp.take(own_real, rows_used, axis=1)
    slot_tags = jnp.take(real_tags, rows_used, axis=0)
    synth_pot = jnp.zeros((marginals, blocks, BLOCK), jnp.float32)
    real_pot = jnp.zeros((marginals, blocks, BLOCK), jnp.float32)
    for sweep_index in range(ITERS):
        if sweep_index == 0:
            panel_rows = jnp.zeros((marginals, slot_count, BLOCK), jnp.float32)
        else:
            panel_rows = fetch_panel(synth_pot, requested, global_col)
        highest, mass_sum = sweep(slot_x, slot_tags, far_y, far_tags, panel_rows, True, group_size)
        highest = jnp.where(usable, highest, SENTINEL)
        mass_sum = jnp.where(usable, mass_sum, 0.0)
        block_top, summed = fold_blocks(highest, mass_sum, rows_used, blocks)
        block_top, summed = joined((block_top, summed), "sub", join_parts)
        real_pot = finish(log_real, block_top, summed)
        own_rows = jnp.take(real_pot, rows_used, axis=1)
        highest, mass_sum = sweep(slot_x, slot_tags, far_y, far_tags, own_rows, False, group_size)
        highest = jnp.where(usable, highest, SENTINEL)
        mass_sum = jnp.where(usable, mass_sum, 0.0)
        synth_pot = column_update(highest, mass_sum, requested, log_synth)
    return (real_pot.reshape(marginals, point_count), synth_pot.reshape(marginals, point_count))


def solution(mesh):
    placed = (
        P(None, ("slab", "blk")),
        P(None, ("slab", "blk")),
        P(("slab", "blk")),
        P(("slab", "blk")),
        P("bag", ("slab", "blk")),
        P("bag", ("slab", "blk")),
        P(("slab", "blk", "sub"), None),
        P(("slab", "blk", "sub"), None),
        P(("slab", "blk", "sub")),
    )
    return jax.shard_map(
        shards,
        mesh=mesh,
        in_specs=placed,
        out_specs=(P("bag", ("slab", "blk")), P("bag", ("slab", "blk"))),
        check_vma=False,
    )
```

profile of v0, /device:TPU:0, one launch (start us, length us, event | category | flops | bytes accessed | tf_op | source)
XLA Modules:
  0.0 132.3 jit_solution(11505282491066260187)
XLA Ops:
  0.7 0.8 select_bitcast_fusion.5
  2.1 6.3 %all-to-all-start = ((s32[4,1,2]{2,1,0:T(1,128)}), s32[4,1,2]{2,1,0:T(1,128)S(1)}, u32[]{:S(2)}, u32[]{:S(2)}) async-start(s32[4,1,2]{2,1,0:T(1,128)} %copy.188), calls=%async_computation | async-start | bytes 4096 | tf_op jit(solution)/shard_map/all_to_all | solution.py:153
  11.5 2.3 %all-to-all-done = s32[4,1,2]{2,1,0:T(1,128)S(1)} async-done(((s32[4,1,2]{2,1,0:T(1,128)}), s32[4,1,2]{2,1,0:T(1,128)S(1)}, u32[]{:S(2)}, u32[]{:S(2)}) %all-to-all-start) | async-done | bytes 64 | tf_op jit(solution)/shard_map/all_to_all | solution.py:153
  15.4 0.7 select_bitcast_fusion
  16.8 3.2 %all-to-all-start.2 = ((bf16[1,4,2,128]{3,2,0,1:T(2,128)(2,1)}), bf16[1,4,2,128]{3,2,0,1:T(2,128)(2,1)S(1)}, u32[]{:S(2)}, u32[]{:S(2)}) async-start(bf16[1,4,2,128]{3,2,0,1:T(2,128)(2,1)} %broadcast_select_fusion.4), calls=%async_computation.2 | async-start | bytes 4096 | tf_op jit(solution)/shard_map/all_to_all | solution.py:158
  20.6 0.7 reduce.4
  21.5 4.0 %all-to-all-done.2 = bf16[1,4,2,128]{3,2,0,1:T(2,128)(2,1)S(1)} async-done(((bf16[1,4,2,128]{3,2,0,1:T(2,128)(2,1)}), bf16[1,4,2,128]{3,2,0,1:T(2,128)(2,1)S(1)}, u32[]{:S(2)}, u32[]{:S(2)}) %all-to-all-start.2) | async-done | bytes 2080 | tf_op jit(solution)/shard_map/all_to_all | solution.py:158
  25.5 3.3 %all-to-all-start.1 = ((bf16[64,4,2,128]{3,0,2,1:T(8,128)(2,1)}), bf16[64,4,2,128]{3,0,2,1:T(8,128)(2,1)S(1)}, u32[]{:S(2)}, u32[]{:S(2)}) async-start(bf16[64,4,2,128]{3,0,2,1:T(8,128)(2,1)} %select_bitcast_fusion), calls=%async_computation.1 | async-start | bytes 262144 | tf_op jit(solution)/shard_map/all_to_all | solution.py:155
  28.8 5.9 %all-to-all-done.1 = bf16[64,4,2,128]{3,0,2,1:T(8,128)(2,1)S(1)} async-done(((bf16[64,4,2,128]{3,0,2,1:T(8,128)(2,1)}), bf16[64,4,2,128]{3,0,2,1:T(8,128)(2,1)S(1)}, u32[]{:S(2)}, u32[]{:S(2)}) %all-to-all-start.1) | async-done | bytes 131104 | tf_op jit(solution)/shard_map/all_to_all | solution.py:155
  34.7 6.2 %while.8 = (s32[]{:T(128)}, f32[2,16,4,128]{3,1,2,0:T(8,128)S(1)}, f32[2,16,4,128]{3,1,2,0:T(8,128)S(1)}, s32[2]{0:T(128)S(1)}, bf16[64,8,128]{2,0,1:T(8,128)(2,...) while((s32[]{:T(128)}, f32[2,16,4,128]{3,1,2,0:T(8,128)S(1)}, ...), condition=%wide.region_5.6_spmd, body=%wide.region_0.5_spmd.sunk | while | flops 11197958 | bytes 1471679 | solution.py:81
  36.5 1.3 exponential_reduce_fusion.8
  39.6 1.3 exponential_reduce_fusion.8
  41.2 1.9 %all-gather.1 = f32[32,8,128]{2,0,1:T(8,128)S(1)} all-gather(f32[16,8,128]{2,0,1:T(8,128)S(1)} %copy.203), channel_id=3, replica_groups=mesh['slab'=2,'blk'=4,'bag'=2,'sub'=2] {'sub'}, dimensions={0}, use_global_device_ids=true | all-gather | bytes 196608 | tf_op jit(solution)/shard_map/all_gather | solution.py:18
  43.9 1.9 %all-gather = f32[32,8,128]{2,0,1:T(8,128)S(1)} all-gather(f32[16,8,128]{2,0,1:T(8,128)S(1)} %copy.205), channel_id=2, replica_groups=mesh['slab'=2,'blk'=4,'bag'=2,'sub'=2] {'sub'}, dimensions={0}, use_global_device_ids=true | all-gather | bytes 196608 | tf_op jit(solution)/shard_map/all_gather | solution.py:18
  46.6 8.7 %while.9 = (s32[]{:T(128)}, f32[2,16,4,128]{3,1,2,0:T(8,128)S(1)}, f32[2,16,4,128]{3,1,2,0:T(8,128)S(1)}, s32[2]{0:T(128)S(1)}, f32[16,8,128]{2,0,1:T(8,128)S(1)...) while((s32[]{:T(128)}, f32[2,16,4,128]{3,1,2,0:T(8,128)S(1)}, ...), condition=%wide.region_13.15_spmd, body=%wide.region_8.14_spmd.sunk | while | flops 16236550 | bytes 1498315 | solution.py:81
  48.2 1.3 fusion.75
  49.5 1.3 %exponential_reduce_fusion.9 = f32[16,4,128]{2,1,0:T(4,128)S(1)} fusion(f32[16,4,128]{2,1,0:T(4,128)S(1)} %fusion.75, f32[4,128,128]{2,1,0:T(8,128)S(1)} %fusion.74, f32[16,4,128]{2,1,0:T(4,128)S(1)} %copy.313), kind=kLoop, calls=%fused_computation.27.clone.1 | loop fusion | flops 4186112 | bytes 360448 | tf_op jit(solution)/shard_map/while/body/eval_jaxpr/reduce_sum | solution.py:78
  52.6 1.3 fusion.75
  53.9 1.3 %exponential_reduce_fusion.9 = f32[16,4,128]{2,1,0:T(4,128)S(1)} fusion(f32[16,4,128]{2,1,0:T(4,128)S(1)} %fusion.75, f32[4,128,128]{2,1,0:T(8,128)S(1)} %fusion.74, f32[16,4,128]{2,1,0:T(4,128)S(1)} %copy.313), kind=kLoop, calls=%fused_computation.27.clone.1 | loop fusion | flops 4186112 | bytes 360448 | tf_op jit(solution)/shard_map/while/body/eval_jaxpr/reduce_sum | solution.py:78
  55.3 0.7 broadcast_select_fusion.1
  56.0 3.3 %all-to-all-start.4 = ((f32[16,4,2,128]{3,0,2,1:T(8,128)}), f32[16,4,2,128]{3,0,2,1:T(8,128)S(1)}, u32[]{:S(2)}, u32[]{:S(2)}) async-start(f32[16,4,2,128]{3,0,2,1:T(8,128)} %get-tuple-element.447), calls=%async_computation.4 | async-start | bytes 131072 | tf_op jit(solution)/shard_map/all_to_all | solution.py:98
  59.3 5.7 %all-to-all-done.4 = f32[16,4,2,128]{3,0,2,1:T(8,128)S(1)} async-done(((f32[16,4,2,128]{3,0,2,1:T(8,128)}), f32[16,4,2,128]{3,0,2,1:T(8,128)S(1)}, u32[]{:S(2)}, u32[]{:S(2)}) %all-to-all-start.4) | async-done | bytes 65568 | tf_op jit(solution)/shard_map/all_to_all | solution.py:98
  65.0 3.3 %all-to-all-start.3 = ((f32[16,4,2,128]{3,0,2,1:T(8,128)}), f32[16,4,2,128]{3,0,2,1:T(8,128)S(1)}, u32[]{:S(2)}, u32[]{:S(2)}) async-start(f32[16,4,2,128]{3,0,2,1:T(8,128)} %get-tuple-element.448), calls=%async_computation.3 | async-start | bytes 131072 | tf_op jit(solution)/shard_map/all_to_all | solution.py:105
  69.0 1.9 %all-gather.3 = f32[32,8,128]{2,0,1:T(8,128)S(1)} all-gather(f32[16,8,128]{2,0,1:T(8,128)S(1)} %copy.212), channel_id=5, replica_groups=mesh['slab'=2,'blk'=4,'bag'=2,'sub'=2] {'sub'}, dimensions={0}, use_global_device_ids=true | all-gather | bytes 196608 | tf_op jit(solution)/shard_map/all_gather | solution.py:18
  70.9 3.1 %all-to-all-done.3 = f32[16,4,2,128]{3,0,2,1:T(8,128)S(1)} async-done(((f32[16,4,2,128]{3,0,2,1:T(8,128)}), f32[16,4,2,128]{3,0,2,1:T(8,128)S(1)}, u32[]{:S(2)}, u32[]{:S(2)}) %all-to-all-start.3) | async-done | bytes 65568 | tf_op jit(solution)/shard_map/all_to_all | solution.py:105
  74.3 1.9 %all-gather.2 = f32[32,8,128]{2,0,1:T(8,128)S(1)} all-gather(f32[16,8,128]{2,0,1:T(8,128)S(1)} %copy.214), channel_id=4, replica_groups=mesh['slab'=2,'blk'=4,'bag'=2,'sub'=2] {'sub'}, dimensions={0}, use_global_device_ids=true | all-gather | bytes 196608 | tf_op jit(solution)/shard_map/all_gather | solution.py:18
  76.8 0.7 select_bitcast_fusion.4
  77.5 3.3 %all-to-all-start.5 = ((f32[16,4,2,128]{3,0,2,1:T(8,128)}), f32[16,4,2,128]{3,0,2,1:T(8,128)S(1)}, u32[]{:S(2)}, u32[]{:S(2)}) async-start(f32[16,4,2,128]{3,0,2,1:T(8,128)} %select_bitcast_fusion.4), calls=%async_computation.5 | async-start | bytes 131072 | tf_op jit(solution)/shard_map/all_to_all | solution.py:90
  80.8 5.7 %all-to-all-done.5 = f32[16,4,2,128]{3,0,2,1:T(8,128)S(1)} async-done(((f32[16,4,2,128]{3,0,2,1:T(8,128)}), f32[16,4,2,128]{3,0,2,1:T(8,128)S(1)}, u32[]{:S(2)}, u32[]{:S(2)}) %all-to-all-start.5) | async-done | bytes 65568 | tf_op jit(solution)/shard_map/all_to_all | solution.py:90
  86.6 10.6 %while.10 = (s32[]{:T(128)}, f32[2,16,4,128]{3,1,2,0:T(8,128)S(1)}, f32[2,16,4,128]{3,1,2,0:T(8,128)S(1)}, s32[2]{0:T(128)S(1)}, f32[16,8,128]{2,1,0:T(8,128)S(1...) while((s32[]{:T(128)}, f32[2,16,4,128]{3,1,2,0:T(8,128)S(1)}, ...), condition=%wide.region_21.23_spmd, body=%wide.region_16.22_spmd.sunk | while | flops 16236550 | bytes 1432779 | solution.py:81
  88.3 1.2 fusion.79
  89.4 2.4 %exponential_reduce_fusion.10 = f32[16,4,128]{2,1,0:T(4,128)S(1)} fusion(f32[16,4,128]{2,1,0:T(4,128)S(1)} %fusion.79, f32[4,128,128]{2,1,0:T(8,128)S(1)} %fusion.78, f32[16,4,128]{2,1,0:T(4,128)S(1)} %constant_dynamic-slice_fusion.22), kind=kLoop, calls=%fused_computation.44.clone.1 | loop fusion | flops 4186112 | bytes 360448 | tf_op jit(solution)/shard_map/while/body/eval_jaxpr/reduce_sum | solution.py:74
  93.6 1.2 fusion.79
  94.8 2.4 %exponential_reduce_fusion.10 = f32[16,4,128]{2,1,0:T(4,128)S(1)} fusion(f32[16,4,128]{2,1,0:T(4,128)S(1)} %fusion.79, f32[4,128,128]{2,1,0:T(8,128)S(1)} %fusion.78, f32[16,4,128]{2,1,0:T(4,128)S(1)} %constant_dynamic-slice_fusion.22), kind=kLoop, calls=%fused_computation.44.clone.1 | loop fusion | flops 4186112 | bytes 360448 | tf_op jit(solution)/shard_map/while/body/eval_jaxpr/reduce_sum | solution.py:74
  98.0 1.9 %all-gather.5 = f32[32,8,128]{2,0,1:T(8,128)S(1)} all-gather(f32[16,8,128]{2,0,1:T(8,128)S(1)} %copy.221), channel_id=7, replica_groups=mesh['slab'=2,'blk'=4,'bag'=2,'sub'=2] {'sub'}, dimensions={0}, use_global_device_ids=true | all-gather | bytes 196608 | tf_op jit(solution)/shard_map/all_gather | solution.py:18
  100.2 1.9 %all-gather.4 = f32[32,8,128]{2,0,1:T(8,128)S(1)} all-gather(f32[16,8,128]{2,0,1:T(8,128)S(1)} %copy.223), channel_id=6, replica_groups=mesh['slab'=2,'blk'=4,'bag'=2,'sub'=2] {'sub'}, dimensions={0}, use_global_device_ids=true | all-gather | bytes 196608 | tf_op jit(solution)/shard_map/all_gather | solution.py:18
  102.9 8.7 %while.11 = (s32[]{:T(128)}, f32[2,16,4,128]{3,1,2,0:T(8,128)S(1)}, f32[2,16,4,128]{3,1,2,0:T(8,128)S(1)}, s32[2]{0:T(128)S(1)}, f32[16,8,128]{2,0,1:T(8,128)S(1...) while((s32[]{:T(128)}, f32[2,16,4,128]{3,1,2,0:T(8,128)S(1)}, ...), condition=%wide.region_29.31_spmd, body=%wide.region_24.30_spmd.sunk | while | flops 16236550 | bytes 1498315 | solution.py:81
  104.5 1.3 fusion.83
  105.8 1.3 %exponential_reduce_fusion.11 = f32[16,4,128]{2,1,0:T(4,128)S(1)} fusion(f32[16,4,128]{2,1,0:T(4,128)S(1)} %fusion.83, f32[4,128,128]{2,1,0:T(8,128)S(1)} %fusion.82, f32[16,4,128]{2,1,0:T(4,128)S(1)} %copy.318), kind=kLoop, calls=%fused_computation.61.clone.1 | loop fusion | flops 4186112 | bytes 360448 | tf_op jit(solution)/shard_map/while/body/eval_jaxpr/reduce_sum | solution.py:78
  108.9 1.3 fusion.83
  110.2 1.3 %exponential_reduce_fusion.11 = f32[16,4,128]{2,1,0:T(4,128)S(1)} fusion(f32[16,4,128]{2,1,0:T(4,128)S(1)} %fusion.83, f32[4,128,128]{2,1,0:T(8,128)S(1)} %fusion.82, f32[16,4,128]{2,1,0:T(4,128)S(1)} %copy.318), kind=kLoop, calls=%fused_computation.61.clone.1 | loop fusion | flops 4186112 | bytes 360448 | tf_op jit(solution)/shard_map/while/body/eval_jaxpr/reduce_sum | solution.py:78
  111.5 0.7 broadcast_select_fusion
  112.3 8.1 %all_to_all.50 = f32[16,4,2,128]{3,0,2,1:T(8,128)S(1)} all-to-all(f32[16,4,2,128]{3,0,2,1:T(8,128)S(1)} %get-tuple-element.445), channel_id=1, replica_groups=mesh['slab'=2,'blk'=4,'bag'=2,'sub'=2] {'blk'}, dimensions={1} | all-to-all | bytes 131072 | tf_op jit(solution)/shard_map/all_to_all | solution.py:98
  120.4 3.3 %all-to-all-start.6 = ((f32[16,4,2,128]{3,0,2,1:T(8,128)}), f32[16,4,2,128]{3,0,2,1:T(8,128)S(1)}, u32[]{:S(2)}, u32[]{:S(2)}) async-start(f32[16,4,2,128]{3,0,2,1:T(8,128)} %get-tuple-element.446), calls=%async_computation.6 | async-start | bytes 131072 | tf_op jit(solution)/shard_map/all_to_all | solution.py:105
  124.4 1.9 %all-gather.7 = f32[32,8,128]{2,1,0:T(8,128)S(1)} all-gather(f32[16,8,128]{2,1,0:T(8,128)S(1)} %select_reduce_fusion.1), channel_id=9, replica_groups=mesh['slab'=2,'blk'=4,'bag'=2,'sub'=2] {'sub'}, dimensions={0}, use_global_device_ids=true | all-gather | bytes 196608 | tf_op jit(solution)/shard_map/all_gather | solution.py:18
  126.3 3.1 %all-to-all-done.6 = f32[16,4,2,128]{3,0,2,1:T(8,128)S(1)} async-done(((f32[16,4,2,128]{3,0,2,1:T(8,128)}), f32[16,4,2,128]{3,0,2,1:T(8,128)S(1)}, u32[]{:S(2)}, u32[]{:S(2)}) %all-to-all-start.6) | async-done | bytes 65568 | tf_op jit(solution)/shard_map/all_to_all | solution.py:105
  129.6 1.9 %all-gather.6 = f32[32,8,128]{2,1,0:T(8,128)S(1)} all-gather(f32[16,8,128]{2,1,0:T(8,128)S(1)} %select_reduce_fusion), channel_id=8, replica_groups=mesh['slab'=2,'blk'=4,'bag'=2,'sub'=2] {'sub'}, dimensions={0}, use_global_device_ids=true | all-gather | bytes 196608 | tf_op jit(solution)/shard_map/all_gather | solution.py:18
  131.5 0.8 fusion.28
  (181 shorter events, 20.8 us)
Async XLA Ops:
  0.6 8.8 %copy-start = (bf16[64,1024]{1,0:T(8,128)(2,1)S(1)}, bf16[64,1024]{1,0:T(8,128)(2,1)}, u32[]{:S(2)}) copy-start(bf16[64,1024]{1,0:T(8,128)(2,1)} %param.19) | copy-start | bytes 393220
  0.6 8.8 %copy-start.4 = (s32[1024]{0:T(1024)S(1)}, s32[1024]{0:T(1024)}, u32[]{:S(2)}) copy-start(s32[1024]{0:T(1024)} %param.21) | copy-start | bytes 12292
  2.1 11.8 %all-to-all-start = ((s32[4,1,2]{2,1,0:T(1,128)}), s32[4,1,2]{2,1,0:T(1,128)S(1)}, u32[]{:S(2)}, u32[]{:S(2)}) async-start(s32[4,1,2]{2,1,0:T(1,128)} %copy.188), calls=%async_computation | async-start | bytes 4096 | tf_op jit(solution)/shard_map/all_to_all | solution.py:153
  9.5 1.3 %copy-start.3 = (bf16[64,1024]{1,0:T(8,128)(2,1)S(1)}, bf16[64,1024]{1,0:T(8,128)(2,1)}, u32[]{:S(2)}) copy-start(bf16[64,1024]{1,0:T(8,128)(2,1)} %param.20) | copy-start | bytes 393220
  10.6 0.7 copy-start.5
  16.8 8.7 %all-to-all-start.2 = ((bf16[1,4,2,128]{3,2,0,1:T(2,128)(2,1)}), bf16[1,4,2,128]{3,2,0,1:T(2,128)(2,1)S(1)}, u32[]{:S(2)}, u32[]{:S(2)}) async-start(bf16[1,4,2,128]{3,2,0,1:T(2,128)(2,1)} %broadcast_select_fusion.4), calls=%async_computation.2 | async-start | bytes 4096 | tf_op jit(solution)/shard_map/all_to_all | solution.py:158
  25.5 9.2 %all-to-all-start.1 = ((bf16[64,4,2,128]{3,0,2,1:T(8,128)(2,1)}), bf16[64,4,2,128]{3,0,2,1:T(8,128)(2,1)S(1)}, u32[]{:S(2)}, u32[]{:S(2)}) async-start(bf16[64,4,2,128]{3,0,2,1:T(8,128)(2,1)} %select_bitcast_fusion), calls=%async_computation.1 | async-start | bytes 262144 | tf_op jit(solution)/shard_map/all_to_all | solution.py:155
  43.8 2.0 %copy-start.1 = (s32[16,1024]{1,0:T(8,128)S(1)}, s32[16,1024]{1,0:T(8,128)}, u32[]{:S(2)}) copy-start(s32[16,1024]{1,0:T(8,128)} %param.23) | copy-start | bytes 196612
  56.0 9.0 %all-to-all-start.4 = ((f32[16,4,2,128]{3,0,2,1:T(8,128)}), f32[16,4,2,128]{3,0,2,1:T(8,128)S(1)}, u32[]{:S(2)}, u32[]{:S(2)}) async-start(f32[16,4,2,128]{3,0,2,1:T(8,128)} %get-tuple-element.447), calls=%async_computation.4 | async-start | bytes 131072 | tf_op jit(solution)/shard_map/all_to_all | solution.py:98
  65.0 9.0 %all-to-all-start.3 = ((f32[16,4,2,128]{3,0,2,1:T(8,128)}), f32[16,4,2,128]{3,0,2,1:T(8,128)S(1)}, u32[]{:S(2)}, u32[]{:S(2)}) async-start(f32[16,4,2,128]{3,0,2,1:T(8,128)} %get-tuple-element.448), calls=%async_computation.3 | async-start | bytes 131072 | tf_op jit(solution)/shard_map/all_to_all | solution.py:105
  74.1 2.0 %copy-start.2 = (s32[16,1024]{1,0:T(8,128)S(1)}, s32[16,1024]{1,0:T(8,128)}, u32[]{:S(2)}) copy-start(s32[16,1024]{1,0:T(8,128)} %param.24) | copy-start | bytes 196612
  77.5 9.0 %all-to-all-start.5 = ((f32[16,4,2,128]{3,0,2,1:T(8,128)}), f32[16,4,2,128]{3,0,2,1:T(8,128)S(1)}, u32[]{:S(2)}, u32[]{:S(2)}) async-start(f32[16,4,2,128]{3,0,2,1:T(8,128)} %select_bitcast_fusion.4), calls=%async_computation.5 | async-start | bytes 131072 | tf_op jit(solution)/shard_map/all_to_all | solution.py:90
  120.4 9.0 %all-to-all-start.6 = ((f32[16,4,2,128]{3,0,2,1:T(8,128)}), f32[16,4,2,128]{3,0,2,1:T(8,128)S(1)}, u32[]{:S(2)}, u32[]{:S(2)}) async-start(f32[16,4,2,128]{3,0,2,1:T(8,128)} %get-tuple-element.446), calls=%async_computation.6 | async-start | bytes 131072 | tf_op jit(solution)/shard_map/all_to_all | solution.py:105
where the time goes:
time: 133 us; the launch traced here: 132 us
  waiting for transfers between devices  29.7 us (22%)
  other arithmetic  29.2 us (22%)
  starting transfers between devices  26 us (20%)
  blocking collectives  23.3 us (18%)
  local copies, waits for them, and re-layouts  14.6 us (11%)
  loops' own time  5.91 us (4%)
  matrix products  2.3 us (2%)
    all_gather x8, blocking collectives, joined(): pieces = jax.tree.map(lambda part: lax.all_gather(part, axis), value)  15.2 us
    all_to_all x1, blocking collectives, column_update(): lax.all_to_all(highest.reshape(marginals, peer_count, capacity, width_pts...  8.1 us
    reduce_sum x4, other arithmetic, one_group(): mass_sum = jnp.sum(jnp.exp(scores - highest[:, :, :, None]), axis=3)  7.43 us
    all_to_all x2, starting transfers between devices, column_update(): lax.all_to_all(mass_sum.reshape(marginals, peer_count, capacity, width_pt...  6.57 us
    all_to_all x1, starting transfers between devices, shards(): lax.all_to_all(wanted, 'blk', split_axis=0, concat_axis=0, tiled=True)  6.32 us
    all_to_all x2, waiting for transfers between devices, column_update(): lax.all_to_all(mass_sum.reshape(marginals, peer_count, capacity, width_pt...  6.15 us
    another operation x4, loops' own time, sweep(): lax.map(one_group, jnp.arange(group_total, dtype=jnp.int32))  5.91 us
    all_to_all x1, waiting for transfers between devices, shards(): lax.all_to_all(jnp.take(own_synth, requested, axis=1), 'blk', split_axis=...  5.87 us
  transfers between devices with their start and end apart: 7, of which 7 were waited for; matrix products, arithmetic and copies ran while one was open for 4% of the time, Pallas kernels for 0%

commit v1 on v0

v1 whole, which is shorter than its diff:
```python
import functools
import math

import jax
import jax.numpy as jnp
import ml_dtypes
from jax import lax
from jax.experimental import pallas as pl
from jax.experimental.pallas import tpu as pltpu
from jax.sharding import PartitionSpec as P

BLOCK = 128
SMOOTH = 0.1
PENALTY = 0.3
SENTINEL = -1e30
ALPHA = 1.0 / (SMOOTH * math.log(2.0))
HIGH = float(ml_dtypes.bfloat16(PENALTY))
LOW = float(ml_dtypes.bfloat16(PENALTY - HIGH))
TILE = 16
MESH = pl.DeviceIdType.MESH
F32 = jnp.float32
BF16 = jnp.bfloat16


def split3(value):
    first = value.astype(BF16).astype(F32)
    second = (value - first).astype(BF16).astype(F32)
    third = (value - first - second).astype(BF16).astype(F32)
    return first, second, third


def put_rows(tile, value, start):
    row = lax.broadcasted_iota(jnp.int32, tile.shape, 0)
    for offset, part in enumerate(split3(value)):
        tile = jnp.where(row == start + offset, part, tile)
    return tile


def fold_max(tops, masks):
    best = jnp.full((masks[0].shape[0], BLOCK), SENTINEL, F32)
    for top, mask in zip(tops, masks):
        best = jnp.maximum(best, jnp.where(mask, top, SENTINEL))
    return best


def kernel(
    peers, cap, blocks, marginals, feats,
    x_ref, y_ref, xc_ref, yc_ref, xw_ref, yw_ref, pb_ref, pr_ref, pc_ref,
    real_out, synth_out,
    xf, xt, xu, wr, ys, req_out, req_in, y_out, y_in,
    s1_out, s1_in, c_out, c_in, own_a, own_t, rep_out, rep_in, s2_out, s2_in, bw,
    big_send, big_recv, send, recv, s_send, s_recv,
):
    slab, blk, bag, sub = (lax.axis_index(name) for name in ("slab", "blk", "bag", "sub"))
    other = 1 - sub
    mine = sub * peers + blk
    group = 2 * peers

    def device(p, s):
        return (slab, p, bag, s)

    others = [(lax.rem(blk + d, peers), s) for d in range(1, peers) for s in (sub, other)]
    others.append((blk, other))

    barrier = pltpu.get_barrier_semaphore()
    for p, s in others:
        pl.semaphore_signal(barrier, inc=1, device_id=device(p, s), device_id_type=MESH)

    for p in range(peers):
        for c in range(cap):
            listed = c < pc_ref[p]
            wanted = jnp.where(listed, pb_ref[p, c], 99).astype(F32)
            req_out[p, c] = jnp.full((TILE, BLOCK), wanted, F32).astype(BF16)
    req_in[mine] = req_out[blk]
    pl.semaphore_wait(barrier, len(others))

    pending = []

    def post(src, dst, send_sem, recv_sem, target):
        copy = pltpu.make_async_remote_copy(
            src_ref=src, dst_ref=dst, send_sem=send_sem, recv_sem=recv_sem,
            device_id=target, device_id_type=MESH,
        )
        copy.start()
        pending.append(copy)

    def arrived(dst, send_sem, recv_sem):
        pltpu.make_async_remote_copy(
            src_ref=dst, dst_ref=dst, send_sem=send_sem, recv_sem=recv_sem,
            device_id=device(blk, other), device_id_type=MESH,
        ).wait_recv()

    for p, s in others:
        post(req_out.at[p], req_in.at[mine], big_send.at[0, s * peers + p], big_recv.at[0, mine],
             device(p, s))

    row = lax.broadcasted_iota(jnp.int32, (TILE, BLOCK), 0)
    cluster = jnp.where(row < 10, row - 6, row - 10)
    for n in range(blocks):
        lanes = slice(n * BLOCK, (n + 1) * BLOCK)
        y = y_ref[:, lanes]
        y32 = y.astype(F32)
        fy = -0.5 * jnp.sum(y32 * y32, axis=0, keepdims=True)
        hit = (row >= 6) & (row < 14) & (cluster == yc_ref[n : n + 1, :])
        tile = jnp.where(hit, jnp.where(row < 10, HIGH, LOW), 0.0)
        tile = jnp.where(row < 3, 1.0, tile)
        tile = put_rows(tile, fy, 3)
        ys[n, 0:feats] = y
        ys[n, feats:] = tile.astype(BF16)
    for n in range(blocks):
        lanes = slice(n * BLOCK, (n + 1) * BLOCK)
        x = x_ref[:, lanes]
        x32 = x.astype(F32)
        fx = -0.5 * jnp.sum(x32 * x32, axis=0, keepdims=True) - PENALTY
        hit = (row >= 6) & (row < 14) & (cluster == xc_ref[n : n + 1, :])
        tile = jnp.where(hit, 1.0, 0.0)
        tile = jnp.where((row >= 3) & (row < 6), 1.0, tile)
        tile = put_rows(tile, fx, 0)
        xf[n] = x
        xt[n] = tile.astype(BF16)
        wr[n] = (xw_ref[:, lanes].astype(F32) + 0.5).astype(BF16)

    def answer(p):
        src = sub * peers + p
        for c in range(cap):
            asked = req_in[src, c]
            value = ys[0].reshape(-1, TILE, BLOCK)
            for n in range(1, blocks):
                value = jnp.where((asked == n)[None], ys[n].reshape(-1, TILE, BLOCK), value)
            yield c, value.reshape(-1, BLOCK)

    for d in range(1, peers):
        p = lax.rem(blk + d, peers)
        src = sub * peers + p
        arrived(req_in.at[src], big_send.at[0, src], big_recv.at[0, src])
        for c, value in answer(p):
            y_out[p, c] = value
        post(y_out.at[p], y_in.at[blk], send.at[0, p], recv.at[0, blk], device(p, sub))
    for c, value in answer(blk):
        y_in[blk, c] = value

    order = [lax.rem(blk + d, peers) for d in range(peers)]
    far_first = order[1:] + order[:1]
    eight = lax.broadcasted_iota(jnp.int32, (blocks, BLOCK), 0)

    def row_of(p, c):
        return pr_ref[p, c]

    def row_mask(p, c):
        return eight == jnp.where(c < pc_ref[p], pr_ref[p, c], blocks)

    contract = (((0,), (0,)), ((), ()))
    slots = [(p, c) for p in order for c in range(cap)]
    masks = [row_mask(p, c) for p, c in slots]

    tops, sums = [], []
    for d, p in enumerate(order):
        if d:
            arrived(y_in.at[p], send.at[0, p], recv.at[0, p])
        for c in range(cap):
            r = row_of(p, c)
            x = jnp.concatenate([xf[r], xt[r]], axis=0)
            z = lax.dot_general(y_in[p, c], x, contract, preferred_element_type=F32)
            top = jnp.max(z, axis=0, keepdims=True)
            tops.append(top)
            sums.append(jnp.sum(jnp.exp2(ALPHA * (z - top)), axis=0, keepdims=True))
    best = fold_max(tops, masks)
    total = jnp.zeros((blocks, BLOCK), F32)
    for top, part, mask in zip(tops, sums, masks):
        total += jnp.where(mask, jnp.exp2(ALPHA * (top - best)) * part, 0.0)
    s1_out[0] = best
    s1_out[1] = total
    post(s1_out, s1_in, s_send.at[0], s_recv.at[0], device(blk, other))
    arrived(s1_in, s_send.at[0], s_recv.at[0])
    peak = jnp.maximum(best, s1_in[0])
    total = total * jnp.exp2(ALPHA * (best - peak)) + s1_in[1] * jnp.exp2(ALPHA * (s1_in[0] - peak))
    used = peak > 0.5 * SENTINEL
    level = jnp.where(used, peak + jnp.log(jnp.where(used, total, 1.0)) * SMOOTH, 0.0)

    def shift_rows(level):
        for n in range(blocks):
            lanes = slice(n * BLOCK, (n + 1) * BLOCK)
            tile = xt[n].astype(F32)
            base = tile[0:1] + tile[1:2] + tile[2:3]
            xu[n] = put_rows(tile, base - level[n : n + 1], 0).astype(BF16)

    def col_sweep(turn, factor):
        for d, p in enumerate(far_first):
            for c in range(cap):
                r = row_of(p, c)
                x = jnp.concatenate([xf[r], xu[r]], axis=0)
                z = lax.dot_general(x, y_in[p, c], contract, preferred_element_type=F32)
                top = jnp.max(z, axis=0, keepdims=True)
                table = jnp.exp2(ALPHA * (z - top)).astype(BF16)
                mass = jnp.dot(factor[r], table, preferred_element_type=F32)
                wide = jnp.broadcast_to(top, (8, BLOCK))
                c_out[turn, p, c, 0:marginals] = mass
                c_out[turn, p, c, marginals:] = wide
                if d == peers - 1:
                    c_in[turn, mine, c, 0:marginals] = mass
                    c_in[turn, mine, c, marginals:] = wide
            for s in (sub, other):
                if d == peers - 1 and s is sub:
                    continue
                post(c_out.at[turn, p], c_in.at[turn, mine], big_send.at[1 + turn, s * peers + p],
                     big_recv.at[1 + turn, mine], device(p, s))

    def col_fold(turn):
        sources = [mine, other * peers + blk]
        sources += [s * peers + p for p in order[1:] for s in (sub, other)]
        tops, hits = [], []
        for d, src in enumerate(sources):
            if d:
                arrived(c_in.at[turn, src], big_send.at[1 + turn, src], big_recv.at[1 + turn, src])
                if turn == 0 and d % 2 == 1:
                    arrived(req_in.at[src], big_send.at[0, src], big_recv.at[0, src])
            for c in range(cap):
                tops.append(c_in[turn, src, c, marginals:][0:1])
                asked = req_in[src, c].astype(F32)[0:1]
                hits.append(asked == eight.astype(F32))
        best = fold_max(tops, hits)
        totals = [jnp.zeros((marginals, BLOCK), F32) for _ in range(blocks)]
        k = 0
        for src in sources:
            for c in range(cap):
                scale = jnp.where(hits[k], jnp.exp2(ALPHA * (tops[k] - best)), 0.0)
                mass = c_in[turn, src, c, 0:marginals]
                for n in range(blocks):
                    totals[n] += scale[n : n + 1] * mass
                k += 1
        return best, totals

    shift_rows(level)
    col_sweep(0, wr)
    best, totals = col_fold(0)
    used = best > 0.5 * SENTINEL
    level = jnp.where(used, best, 0.0)
    for n in range(blocks):
        lanes = slice(n * BLOCK, (n + 1) * BLOCK)
        some = used[n : n + 1]
        weight = yw_ref[:, lanes].astype(F32) + 0.5
        own_a[n] = (weight / jnp.where(some, totals[n], 1.0)).astype(BF16)
        tile = ys[n, feats:].astype(F32)
        base = tile[3:4] + tile[4:5] + tile[5:6]
        own_t[n] = put_rows(tile, base - level[n : n + 1], 3).astype(BF16)
    for d, p in enumerate(far_first):
        src = sub * peers + p
        for c in range(cap):
            asked = req_in[src, c]
            factor, tile = own_a[0], own_t[0]
            for n in range(1, blocks):
                hit = asked == n
                factor = jnp.where(hit, own_a[n], factor)
                tile = jnp.where(hit, own_t[n], tile)
            target = rep_in if d == peers - 1 else rep_out
            target[p, c, 0] = factor
            target[p, c, 1] = tile
        if d < peers - 1:
            post(rep_out.at[p], rep_in.at[blk], send.at[1, p], recv.at[1, blk], device(p, sub))

    tops, masses = [], []
    for d, p in enumerate(order):
        if d:
            arrived(rep_in.at[p], send.at[1, p], recv.at[1, p])
        for c in range(cap):
            r = row_of(p, c)
            x = jnp.concatenate([xf[r], xt[r]], axis=0)
            y = jnp.concatenate([y_in[p, c][0:feats], rep_in[p, c, 1]], axis=0)
            z = lax.dot_general(y, x, contract, preferred_element_type=F32)
            top = jnp.max(z, axis=0, keepdims=True)
            table = jnp.exp2(ALPHA * (z - top)).astype(BF16)
            tops.append(top)
            masses.append(jnp.dot(rep_in[p, c, 0], table, preferred_element_type=F32))
    best = fold_max(tops, masks)
    totals = [jnp.zeros((marginals, BLOCK), F32) for _ in range(blocks)]
    for top, mass, mask in zip(tops, masses, masks):
        scale = jnp.where(mask, jnp.exp2(ALPHA * (top - best)), 0.0)
        for n in range(blocks):
            totals[n] += scale[n : n + 1] * mass
    per = marginals // 8
    for n in range(blocks):
        s2_out[1 + per * n : 1 + per * (n + 1)] = totals[n].reshape(per, 8, BLOCK)
    s2_out[0] = best
    post(s2_out, s2_in, s_send.at[1], s_recv.at[1], device(blk, other))
    arrived(s2_in, s_send.at[1], s_recv.at[1])
    theirs = s2_in[0]
    peak = jnp.maximum(best, theirs)
    scale_own, scale_far = jnp.exp2(ALPHA * (best - peak)), jnp.exp2(ALPHA * (theirs - peak))
    used = peak > 0.5 * SENTINEL
    level = jnp.where(used, peak, 0.0)
    sums = []
    for n in range(blocks):
        lanes = slice(n * BLOCK, (n + 1) * BLOCK)
        far = s2_in[1 + per * n : 1 + per * (n + 1)].reshape(marginals, BLOCK)
        total = totals[n] * scale_own[n : n + 1] + far * scale_far[n : n + 1]
        total = jnp.where(used[n : n + 1], total, 1.0)
        weight = xw_ref[:, lanes].astype(F32) + 0.5
        bw[n] = (weight / total).astype(BF16)
        sums.append(total)
    shift_rows(level)
    col_sweep(1, bw)
    for n in range(blocks):
        lanes = slice(n * BLOCK, (n + 1) * BLOCK)
        weight = xw_ref[:, lanes].astype(F32) + 0.5
        real_out[:, lanes] = SMOOTH * (jnp.log(weight) - jnp.log(sums[n])) - level[n : n + 1]
    best, totals = col_fold(1)
    used = best > 0.5 * SENTINEL
    level = jnp.where(used, best, 0.0)
    for n in range(blocks):
        lanes = slice(n * BLOCK, (n + 1) * BLOCK)
        weight = yw_ref[:, lanes].astype(F32) + 0.5
        total = jnp.where(used[n : n + 1], totals[n], 1.0)
        synth_out[:, lanes] = SMOOTH * (jnp.log(weight) - jnp.log(total)) - level[n : n + 1]
    for copy in pending:
        copy.wait_send()


def shards(
    real_points, synth_points, real_cluster, synth_cluster, real_weight, synth_weight,
    pair_block, pair_row, pair_count,
):
    feats, count = real_points.shape
    blocks = count // BLOCK
    kept = real_weight.shape[0]
    marginals = -(-kept // TILE) * TILE
    if marginals > kept:
        grow = ((0, marginals - kept), (0, 0))
        real_weight, synth_weight = jnp.pad(real_weight, grow), jnp.pad(synth_weight, grow)
    peers, cap = pair_block.shape
    group = 2 * peers
    depth = feats + TILE
    vmem = pl.BlockSpec(memory_space=pltpu.VMEM)
    smem = pl.BlockSpec(memory_space=pltpu.SMEM)
    real_pot, synth_pot = pl.pallas_call(
        functools.partial(kernel, peers, cap, blocks, marginals, feats),
        out_shape=(
            jax.ShapeDtypeStruct((marginals, count), F32),
            jax.ShapeDtypeStruct((marginals, count), F32),
        ),
        in_specs=[vmem] * 6 + [smem] * 3,
        out_specs=(vmem, vmem),
        scratch_shapes=[
            pltpu.VMEM((blocks, feats, BLOCK), BF16),
            pltpu.VMEM((blocks, TILE, BLOCK), BF16),
            pltpu.VMEM((blocks, TILE, BLOCK), BF16),
            pltpu.VMEM((blocks, marginals, BLOCK), BF16),
            pltpu.VMEM((blocks, depth, BLOCK), BF16),
            pltpu.VMEM((peers, cap, TILE, BLOCK), BF16),
            pltpu.VMEM((group, cap, TILE, BLOCK), BF16),
            pltpu.VMEM((peers, cap, depth, BLOCK), BF16),
            pltpu.VMEM((peers, cap, depth, BLOCK), BF16),
            pltpu.VMEM((2, blocks, BLOCK), F32),
            pltpu.VMEM((2, blocks, BLOCK), F32),
            pltpu.VMEM((2, peers, cap, marginals + 8, BLOCK), F32),
            pltpu.VMEM((2, group, cap, marginals + 8, BLOCK), F32),
            pltpu.VMEM((blocks, marginals, BLOCK), BF16),
            pltpu.VMEM((blocks, TILE, BLOCK), BF16),
            pltpu.VMEM((peers, cap, 2, TILE, BLOCK), BF16),
            pltpu.VMEM((peers, cap, 2, TILE, BLOCK), BF16),
            pltpu.VMEM((1 + marginals // 8 * blocks, 8, BLOCK), F32),
            pltpu.VMEM((1 + marginals // 8 * blocks, 8, BLOCK), F32),
            pltpu.VMEM((blocks, marginals, BLOCK), BF16),
            pltpu.SemaphoreType.DMA((3, group)),
            pltpu.SemaphoreType.DMA((3, group)),
            pltpu.SemaphoreType.DMA((2, peers)),
            pltpu.SemaphoreType.DMA((2, peers)),
            pltpu.SemaphoreType.DMA((2,)),
            pltpu.SemaphoreType.DMA((2,)),
        ],
        compiler_params=pltpu.CompilerParams(
            collective_id=0, has_side_effects=True, vmem_limit_bytes=32 * 1024 * 1024
        ),
    )(
        real_points, synth_points,
        real_cluster.reshape(blocks, BLOCK), synth_cluster.reshape(blocks, BLOCK),
        real_weight, synth_weight, pair_block, pair_row, pair_count,
    )
    return real_pot[:kept], synth_pot[:kept]


def solution(mesh):
    placed = (
        P(None, ("slab", "blk")),
        P(None, ("slab", "blk")),
        P(("slab", "blk")),
        P(("slab", "blk")),
        P("bag", ("slab", "blk")),
        P("bag", ("slab", "blk")),
        P(("slab", "blk", "sub"), None),
        P(("slab", "blk", "sub"), None),
        P(("slab", "blk", "sub")),
    )
    return jax.shard_map(
        shards,
        mesh=mesh,
        in_specs=placed,
        out_specs=(P("bag", ("slab", "blk")), P("bag", ("slab", "blk"))),
        check_vma=False,
    )
```

time: 133 us -> 42.4 us (0.32)
  Pallas kernels: 0 us -> 35.2 us
  waiting for transfers between devices: 29.7 us -> 0 us
  other arithmetic: 29.2 us -> 0 us
  starting transfers between devices: 26 us -> 0 us
  blocking collectives: 23.3 us -> 0 us
  local copies, waits for them, and re-layouts: 14.6 us -> 6.19 us
  loops' own time: 5.91 us -> 0 us
  matrix products: 2.3 us -> 0 us
    pallas_call x0 -> x1, Pallas kernels: none -> 35.2 us  [shards(): pl.pallas_call(functools.partial(kernel, peers, cap, blocks, marginals, f...]
    all_to_all x7 -> x0, waiting for transfers between devices: 29.7 us -> none  [the longest x2 6.15 us: column_update(): lax.all_to_all(mass_sum.reshape(marginals, peer_count, capacity, width_pt...]
    all_to_all x7 -> x0, starting transfers between devices: 26 us -> none  [the longest x2 6.57 us: column_update(): lax.all_to_all(mass_sum.reshape(marginals, peer_count, capacity, width_pt...]
    all_gather x8 -> x0, blocking collectives: 15.2 us -> none  [joined(): pieces = jax.tree.map(lambda part: lax.all_gather(part, axis), value)]
    reduce_sum x20 -> x0, other arithmetic: 13.6 us -> none  [the longest x4 7.43 us: one_group(): mass_sum = jnp.sum(jnp.exp(scores - highest[:, :, :, None]), axis=3)]
    all_to_all x1 -> x0, blocking collectives: 8.1 us -> none  [column_update(): lax.all_to_all(highest.reshape(marginals, peer_count, capacity, width_pts...]
    reduce_max x10 -> x0, other arithmetic: 7.91 us -> none  [the longest x4 5.09 us: one_group(): highest = jnp.max(scores, axis=2)]
    gather x11 -> x0, local copies, waits for them, and re-layouts: 6.16 us -> none  [the longest x4 2.22 us: fold_blocks(): slot_top = jnp.take(block_top, owners, axis=1)]
  transfers between devices with their start and end apart: 7 -> 0, of which waited for: 7 -> 0; matrix products, arithmetic and copies ran while one was open for 4% -> 0% of each run, Pallas kernels for 0% -> 0%
where the time goes in v1:
time: 42.4 us; the launch traced here: 42.1 us
  Pallas kernels  35.2 us (83%)
  local copies, waits for them, and re-layouts  6.19 us (15%)
  between operations  0.67 us (2%)
    pallas_call x1, Pallas kernels, shards(): pl.pallas_call(functools.partial(kernel, peers, cap, blocks, marginals, f...  35.2 us
    unnamed x20, local copies, waits for them, and re-layouts  6.19 us

profile of v1, /device:TPU:0, one launch (start us, length us, event | category | flops | bytes accessed | tf_op | source)
XLA Modules:
  0.0 42.1 jit_solution(6896552662593494368)
XLA Ops:
  0.6 0.0 copy-start.7
  0.6 0.0 copy-start.5
  0.7 0.0 copy-start.4
  0.7 0.8 %copy.11.pb_ref = s32[4,2]{1,0:T(4,128)S(1)} copy(s32[4,2]{0,1:T(2,128)} %param.15) | data formatting | bytes 64 | tf_op args[6]
  1.4 0.0 copy-done.7
  1.4 0.0 copy-start.6
  1.4 0.1 copy.12.pr_ref
  1.5 0.0 copy-done.5
  1.5 0.0 copy-done.4
  1.5 0.6 %copy-done.6 = s32[4]{0:T(128)S(1)} copy-done((s32[4]{0:T(128)S(1)}, s32[4]{0:T(128)}, u32[]{:S(2)}) %copy-start.6) | copy-done | bytes 40
  2.1 0.0 copy-start
  2.1 0.9 %copy-done = bf16[64,1024]{1,0:T(8,128)(2,1)S(1)} copy-done((bf16[64,1024]{1,0:T(8,128)(2,1)S(1)}, bf16[64,1024]{1,0:T(8,128)(2,1)}, u32[]{:S(2)}) %copy-start) | copy-done | bytes 131096
  3.0 0.0 copy-start.1
  3.0 0.9 %copy-done.1 = bf16[64,1024]{1,0:T(8,128)(2,1)S(1)} copy-done((bf16[64,1024]{1,0:T(8,128)(2,1)S(1)}, bf16[64,1024]{1,0:T(8,128)(2,1)}, u32[]{:S(2)}) %copy-start.1) | copy-done | bytes 131096
  3.9 0.0 copy-start.2
  3.9 0.8 %copy-done.2 = s32[16,1024]{1,0:T(8,128)S(1)} copy-done((s32[16,1024]{1,0:T(8,128)S(1)}, s32[16,1024]{1,0:T(8,128)}, u32[]{:S(2)}) %copy-start.2) | copy-done | bytes 65560
  4.8 0.0 copy-start.3
  4.8 0.8 %copy-done.3 = s32[16,1024]{1,0:T(8,128)S(1)} copy-done((s32[16,1024]{1,0:T(8,128)S(1)}, s32[16,1024]{1,0:T(8,128)}, u32[]{:S(2)}) %copy-start.3) | copy-done | bytes 65560
  5.6 35.2 %shard_map.104 = (f32[16,1024]{1,0:T(8,128)S(1)}, f32[16,1024]{1,0:T(8,128)S(1)}) custom-call(bf16[64,1024]{1,0:T(8,128)(2,1)S(1)} %copy-done, bf16[64,1024]{1,0:T(8,128)(2,1)S(1)} %copy-done.1, s32[8,128]{1,0:T(8,128)S(1)} %bitcast.2, s32[8,128]{1,0:T(8,128)S(1)} %bitcast.3, s32[16,1024]{1,0:T(8,128)S(1)} %copy-done.2, s32[16,1024]{1,0:T(8,128)S(1)} %copy-done.3, ...), custom_call_target="tpu_custom_call" | custom-call | tf_op jit(solution)/shard_map/pallas_call | solution.py:334
  40.8 0.6 %copy.15 = f32[16,1024]{1,0:T(8,128)} copy(f32[16,1024]{1,0:T(8,128)S(1)} %get-tuple-element.4) | data formatting | bytes 131072
  41.5 0.6 %copy.16 = f32[16,1024]{1,0:T(8,128)} copy(f32[16,1024]{1,0:T(8,128)S(1)} %get-tuple-element.5) | data formatting | bytes 131072
Async XLA Ops:
  0.6 0.8 %copy-start.7 = (s32[4,2]{0,1:T(2,128)S(1)}, s32[4,2]{0,1:T(2,128)}, u32[]{:S(2)}) copy-start(s32[4,2]{0,1:T(2,128)} %param.16) | copy-start | bytes 100
  0.6 0.9 %copy-start.5 = (s32[1024]{0:T(1024)S(1)}, s32[1024]{0:T(1024)}, u32[]{:S(2)}) copy-start(s32[1024]{0:T(1024)} %param.12) | copy-start | bytes 12292
  0.7 0.9 %copy-start.4 = (s32[1024]{0:T(1024)S(1)}, s32[1024]{0:T(1024)}, u32[]{:S(2)}) copy-start(s32[1024]{0:T(1024)} %param.11) | copy-start | bytes 12292
  1.4 0.7 %copy-start.6 = (s32[4]{0:T(128)S(1)}, s32[4]{0:T(128)}, u32[]{:S(2)}) copy-start(s32[4]{0:T(128)} %pc_ref.1) | copy-start | bytes 52
  2.1 0.9 %copy-start = (bf16[64,1024]{1,0:T(8,128)(2,1)S(1)}, bf16[64,1024]{1,0:T(8,128)(2,1)}, u32[]{:S(2)}) copy-start(bf16[64,1024]{1,0:T(8,128)(2,1)} %x_ref.1) | copy-start | bytes 393220
  3.0 0.9 %copy-start.1 = (bf16[64,1024]{1,0:T(8,128)(2,1)S(1)}, bf16[64,1024]{1,0:T(8,128)(2,1)}, u32[]{:S(2)}) copy-start(bf16[64,1024]{1,0:T(8,128)(2,1)} %y_ref.1) | copy-start | bytes 393220
  3.9 0.8 %copy-start.2 = (s32[16,1024]{1,0:T(8,128)S(1)}, s32[16,1024]{1,0:T(8,128)}, u32[]{:S(2)}) copy-start(s32[16,1024]{1,0:T(8,128)} %xw_ref.1) | copy-start | bytes 196612
  4.8 0.8 %copy-start.3 = (s32[16,1024]{1,0:T(8,128)S(1)}, s32[16,1024]{1,0:T(8,128)}, u32[]{:S(2)}) copy-start(s32[16,1024]{1,0:T(8,128)} %yw_ref.1) | copy-start | bytes 196612

commit v2 on v1

--- a/solution.py
+++ b/solution.py
@@ -45,13 +45,23 @@
 
 def kernel(
     peers, cap, blocks, marginals, feats,
-    x_ref, y_ref, xc_ref, yc_ref, xw_ref, yw_ref, pb_ref, pr_ref, pc_ref,
+    x_hbm, y_hbm, xc_hbm, yc_hbm, xw_hbm, yw_hbm, pb_hbm, pr_hbm, pc_hbm,
     real_out, synth_out,
+    x_ref, y_ref, xc_ref, yc_ref, xw_ref, yw_ref, pb_ref, pr_ref, pc_ref, in_sem,
     xf, xt, xu, wr, ys, req_out, req_in, y_out, y_in,
     s1_out, s1_in, c_out, c_in, own_a, own_t, rep_out, rep_in, s2_out, s2_in, bw,
     big_send, big_recv, send, recv, s_send, s_recv,
 ):
     slab, blk, bag, sub = (lax.axis_index(name) for name in ("slab", "blk", "bag", "sub"))
+    loads = [
+        pltpu.make_async_copy(src, dst, in_sem.at[k])
+        for k, (src, dst) in enumerate((
+            (pb_hbm, pb_ref), (pc_hbm, pc_ref), (pr_hbm, pr_ref), (y_hbm, y_ref), (yc_hbm, yc_ref),
+            (x_hbm, x_ref), (xc_hbm, xc_ref), (xw_hbm, xw_ref), (yw_hbm, yw_ref),
+        ))
+    ]
+    for load in loads:
+        load.start()
     other = 1 - sub
     mine = sub * peers + blk
     group = 2 * peers
@@ -66,10 +76,12 @@
     for p, s in others:
         pl.semaphore_signal(barrier, inc=1, device_id=device(p, s), device_id_type=MESH)
 
+    for load in loads[:3]:
+        load.wait()
     for p in range(peers):
         for c in range(cap):
             listed = c < pc_ref[p]
-            wanted = jnp.where(listed, pb_ref[p, c], 99).astype(F32)
+            wanted = jnp.where(listed, pb_ref[c, p], 99).astype(F32)
             req_out[p, c] = jnp.full((TILE, BLOCK), wanted, F32).astype(BF16)
     req_in[mine] = req_out[blk]
     pl.semaphore_wait(barrier, len(others))
@@ -94,6 +106,8 @@
         post(req_out.at[p], req_in.at[mine], big_send.at[0, s * peers + p], big_recv.at[0, mine],
              device(p, s))
 
+    for load in loads[3:]:
+        load.wait()
     row = lax.broadcasted_iota(jnp.int32, (TILE, BLOCK), 0)
     cluster = jnp.where(row < 10, row - 6, row - 10)
     for n in range(blocks):
@@ -144,10 +158,10 @@
     eight = lax.broadcasted_iota(jnp.int32, (blocks, BLOCK), 0)
 
     def row_of(p, c):
-        return pr_ref[p, c]
+        return pr_ref[c, p]
 
     def row_mask(p, c):
-        return eight == jnp.where(c < pc_ref[p], pr_ref[p, c], blocks)
+        return eight == jnp.where(c < pc_ref[p], pr_ref[c, p], blocks)
 
     contract = (((0,), (0,)), ((), ()))
     slots = [(p, c) for p in order for c in range(cap)]
@@ -155,8 +169,9 @@
 
     tops, sums = [], []
     for d, p in enumerate(order):
-        if d:
-            arrived(y_in.at[p], send.at[0, p], recv.at[0, p])
+        if d == 1:
+            for q in order[1:]:
+                arrived(y_in.at[q], send.at[0, q], recv.at[0, q])
         for c in range(cap):
             r = row_of(p, c)
             x = jnp.concatenate([xf[r], xt[r]], axis=0)
@@ -185,7 +200,7 @@
             xu[n] = put_rows(tile, base - level[n : n + 1], 0).astype(BF16)
 
     def col_sweep(turn, factor):
-        for d, p in enumerate(far_first):
+        def masses(p):
             for c in range(cap):
                 r = row_of(p, c)
                 x = jnp.concatenate([xf[r], xu[r]], axis=0)
@@ -193,17 +208,24 @@
                 top = jnp.max(z, axis=0, keepdims=True)
                 table = jnp.exp2(ALPHA * (z - top)).astype(BF16)
                 mass = jnp.dot(factor[r], table, preferred_element_type=F32)
-                wide = jnp.broadcast_to(top, (8, BLOCK))
+                yield c, mass, jnp.broadcast_to(top, (8, BLOCK))
+
+        def deliver(p, s):
+            post(c_out.at[turn, p], c_in.at[turn, mine], big_send.at[1 + turn, s * peers + p],
+                 big_recv.at[1 + turn, mine], device(p, s))
+
+        for p in order[1:]:
+            for c, mass, top in masses(p):
                 c_out[turn, p, c, 0:marginals] = mass
-                c_out[turn, p, c, marginals:] = wide
-                if d == peers - 1:
-                    c_in[turn, mine, c, 0:marginals] = mass
-                    c_in[turn, mine, c, marginals:] = wide
-            for s in (sub, other):
-                if d == peers - 1 and s is sub:
-                    continue
-                post(c_out.at[turn, p], c_in.at[turn, mine], big_send.at[1 + turn, s * peers + p],
-                     big_recv.at[1 + turn, mine], device(p, s))
+                c_out[turn, p, c, marginals:] = top
+        for p in order[1:]:
+            deliver(p, sub)
+            deliver(p, other)
+        for c, mass, top in masses(blk):
+            for target in (c_out.at[turn, blk, c], c_in.at[turn, mine, c]):
+                target[0:marginals] = mass
+                target[marginals:] = top
+        deliver(blk, other)
 
     def col_fold(turn):
         sources = [mine, other * peers + blk]
@@ -260,8 +282,9 @@
 
     tops, masses = [], []
     for d, p in enumerate(order):
-        if d:
-            arrived(rep_in.at[p], send.at[1, p], recv.at[1, p])
+        if d == 1:
+            for q in order[1:]:
+                arrived(rep_in.at[q], send.at[1, q], recv.at[1, q])
         for c in range(cap):
             r = row_of(p, c)
             x = jnp.concatenate([xf[r], xt[r]], axis=0)
@@ -330,16 +353,26 @@
     group = 2 * peers
     depth = feats + TILE
     vmem = pl.BlockSpec(memory_space=pltpu.VMEM)
-    smem = pl.BlockSpec(memory_space=pltpu.SMEM)
+    hbm = pl.BlockSpec(memory_space=pltpu.HBM)
     real_pot, synth_pot = pl.pallas_call(
         functools.partial(kernel, peers, cap, blocks, marginals, feats),
         out_shape=(
             jax.ShapeDtypeStruct((marginals, count), F32),
             jax.ShapeDtypeStruct((marginals, count), F32),
         ),
-        in_specs=[vmem] * 6 + [smem] * 3,
+        in_specs=[hbm] * 9,
         out_specs=(vmem, vmem),
         scratch_shapes=[
+            pltpu.VMEM((feats, count), BF16),
+            pltpu.VMEM((feats, count), BF16),
+            pltpu.VMEM((blocks, BLOCK), jnp.int32),
+            pltpu.VMEM((blocks, BLOCK), jnp.int32),
+            pltpu.VMEM((marginals, count), jnp.int32),
+            pltpu.VMEM((marginals, count), jnp.int32),
+            pltpu.SMEM((cap, peers), jnp.int32),
+            pltpu.SMEM((cap, peers), jnp.int32),
+            pltpu.SMEM((peers,), jnp.int32),
+            pltpu.SemaphoreType.DMA((9,)),
             pltpu.VMEM((blocks, feats, BLOCK), BF16),
             pltpu.VMEM((blocks, TILE, BLOCK), BF16),
             pltpu.VMEM((blocks, TILE, BLOCK), BF16),
@@ -368,12 +401,12 @@
             pltpu.SemaphoreType.DMA((2,)),
         ],
         compiler_params=pltpu.CompilerParams(
-            collective_id=0, has_side_effects=True, vmem_limit_bytes=32 * 1024 * 1024
+            collective_id=0, has_side_effects=True, vmem_limit_bytes=62 * 1024 * 1024
         ),
     )(
         real_points, synth_points,
         real_cluster.reshape(blocks, BLOCK), synth_cluster.reshape(blocks, BLOCK),
-        real_weight, synth_weight, pair_block, pair_row, pair_count,
+        real_weight, synth_weight, pair_block.T, pair_row.T, pair_count,
     )
     return real_pot[:kept], synth_pot[:kept]
 

time: 42.4 us -> 38.8 us (0.915)
  local copies, waits for them, and re-layouts: 6.19 us -> 2.14 us
  Pallas kernels: 35.2 us -> 35.9 us
    unnamed x20 -> x4, local copies, waits for them, and re-layouts: 6.19 us -> 2.14 us
    pallas_call x1, Pallas kernels: 35.2 us -> 35.9 us  [shards(): pl.pallas_call(functools.partial(kernel, peers, cap, blocks, marginals, f...]
where the time goes in v2:
time: 38.8 us; the launch traced here: 38.7 us
  Pallas kernels  35.9 us (93%)
  local copies, waits for them, and re-layouts  2.14 us (6%)
  between operations  0.65 us (2%)
    pallas_call x1, Pallas kernels, shards(): pl.pallas_call(functools.partial(kernel, peers, cap, blocks, marginals, f...  35.9 us
    unnamed x4, local copies, waits for them, and re-layouts  2.14 us

profile of v2, /device:TPU:0, one launch (start us, length us, event | category | flops | bytes accessed | tf_op | source)
XLA Modules:
  0.0 38.7 jit_solution(12048258797494902564)
XLA Ops:
  0.6 35.9 %shard_map.104 = (f32[16,1024]{1,0:T(8,128)}, f32[16,1024]{1,0:T(8,128)}) custom-call(bf16[64,1024]{1,0:T(8,128)(2,1)} %x_hbm.1, bf16[64,1024]{1,0:T(8,128)(2,1)} %y_hbm.1, s32[8,128]{1,0:T(8,128)} %bitcast.4, s32[8,128]{1,0:T(8,128)} %bitcast.5, s32[16,1024]{1,0:T(8,128)} %xw_hbm.1, s32[16,1024]{1,0:T(8,128)} %yw_hbm.1, s32[2,4]{1,0:T(2,128)} %bitcast.6, ...), custom_call_target="tpu_custom_call" | custom-call | tf_op jit(solution)/shard_map/pallas_call | solution.py:357
  36.5 0.0 copy-start
  36.5 1.5 %copy.13 = f32[16,1024]{1,0:T(8,128)} copy(f32[16,1024]{1,0:T(8,128)} %get-tuple-element.4) | data formatting | bytes 131072
  38.0 0.0 copy-done
  38.0 0.6 %copy.14 = f32[16,1024]{1,0:T(8,128)} copy(f32[16,1024]{1,0:T(8,128)S(1)} %copy-done) | data formatting | bytes 131072
Async XLA Ops:
  36.5 1.5 %copy-start = (f32[16,1024]{1,0:T(8,128)S(1)}, f32[16,1024]{1,0:T(8,128)}, u32[]{:S(2)}) copy-start(f32[16,1024]{1,0:T(8,128)} %get-tuple-element.5) | copy-start | bytes 196612

commit v3 on v2

--- a/solution.py
+++ b/solution.py
@@ -82,7 +82,7 @@
         for c in range(cap):
             listed = c < pc_ref[p]
             wanted = jnp.where(listed, pb_ref[c, p], 99).astype(F32)
-            req_out[p, c] = jnp.full((TILE, BLOCK), wanted, F32).astype(BF16)
+            req_out[p, c : c + 1] = jnp.full((1, BLOCK), wanted, F32)
     req_in[mine] = req_out[blk]
     pl.semaphore_wait(barrier, len(others))
 
@@ -106,7 +106,7 @@
         post(req_out.at[p], req_in.at[mine], big_send.at[0, s * peers + p], big_recv.at[0, mine],
              device(p, s))
 
-    for load in loads[3:]:
+    for load in loads[3:5]:
         load.wait()
     row = lax.broadcasted_iota(jnp.int32, (TILE, BLOCK), 0)
     cluster = jnp.where(row < 10, row - 6, row - 10)
@@ -121,6 +121,30 @@
         tile = put_rows(tile, fy, 3)
         ys[n, 0:feats] = y
         ys[n, feats:] = tile.astype(BF16)
+    def asked_block(src, c):
+        return jnp.broadcast_to(req_in[src, c : c + 1], (TILE, BLOCK)).astype(BF16)
+
+    def answer(p):
+        src = sub * peers + p
+        for c in range(cap):
+            asked = asked_block(src, c)
+            value = ys[0].reshape(-1, TILE, BLOCK)
+            for n in range(1, blocks):
+                value = jnp.where((asked == n)[None], ys[n].reshape(-1, TILE, BLOCK), value)
+            yield c, value.reshape(-1, BLOCK)
+
+    for d in range(1, peers):
+        p = lax.rem(blk + d, peers)
+        src = sub * peers + p
+        arrived(req_in.at[src], big_send.at[0, src], big_recv.at[0, src])
+        for c, value in answer(p):
+            y_out[p, c] = value
+        post(y_out.at[p], y_in.at[blk], send.at[0, p], recv.at[0, blk], device(p, sub))
+    for c, value in answer(blk):
+        y_in[blk, c] = value
+
+    for load in loads[5:]:
+        load.wait()
     for n in range(blocks):
         lanes = slice(n * BLOCK, (n + 1) * BLOCK)
         x = x_ref[:, lanes]
@@ -133,25 +157,6 @@
         xf[n] = x
         xt[n] = tile.astype(BF16)
         wr[n] = (xw_ref[:, lanes].astype(F32) + 0.5).astype(BF16)
-
-    def answer(p):
-        src = sub * peers + p
-        for c in range(cap):
-            asked = req_in[src, c]
-            value = ys[0].reshape(-1, TILE, BLOCK)
-            for n in range(1, blocks):
-                value = jnp.where((asked == n)[None], ys[n].reshape(-1, TILE, BLOCK), value)
-            yield c, value.reshape(-1, BLOCK)
-
-    for d in range(1, peers):
-        p = lax.rem(blk + d, peers)
-        src = sub * peers + p
-        arrived(req_in.at[src], big_send.at[0, src], big_recv.at[0, src])
-        for c, value in answer(p):
-            y_out[p, c] = value
-        post(y_out.at[p], y_in.at[blk], send.at[0, p], recv.at[0, blk], device(p, sub))
-    for c, value in answer(blk):
-        y_in[blk, c] = value
 
     order = [lax.rem(blk + d, peers) for d in range(peers)]
     far_first = order[1:] + order[:1]
@@ -208,23 +213,27 @@
                 top = jnp.max(z, axis=0, keepdims=True)
                 table = jnp.exp2(ALPHA * (z - top)).astype(BF16)
                 mass = jnp.dot(factor[r], table, preferred_element_type=F32)
-                yield c, mass, jnp.broadcast_to(top, (8, BLOCK))
+                yield c, mass.astype(BF16), top
 
         def deliver(p, s):
             post(c_out.at[turn, p], c_in.at[turn, mine], big_send.at[1 + turn, s * peers + p],
                  big_recv.at[1 + turn, mine], device(p, s))
 
+        def keep(p, targets):
+            tile = jnp.zeros((TILE, BLOCK), F32)
+            for c, mass, top in masses(p):
+                tile = put_rows(tile, top, 3 * c)
+                for target in targets:
+                    target[c * marginals : (c + 1) * marginals] = mass
+            for target in targets:
+                target[cap * marginals :] = tile.astype(BF16)
+
         for p in order[1:]:
-            for c, mass, top in masses(p):
-                c_out[turn, p, c, 0:marginals] = mass
-                c_out[turn, p, c, marginals:] = top
+            keep(p, [c_out.at[turn, p]])
         for p in order[1:]:
             deliver(p, sub)
             deliver(p, other)
-        for c, mass, top in masses(blk):
-            for target in (c_out.at[turn, blk, c], c_in.at[turn, mine, c]):
-                target[0:marginals] = mass
-                target[marginals:] = top
+        keep(blk, [c_out.at[turn, blk], c_in.at[turn, mine]])
         deliver(blk, other)
 
     def col_fold(turn):
@@ -236,17 +245,17 @@
                 arrived(c_in.at[turn, src], big_send.at[1 + turn, src], big_recv.at[1 + turn, src])
                 if turn == 0 and d % 2 == 1:
                     arrived(req_in.at[src], big_send.at[0, src], big_recv.at[0, src])
+            tile = c_in[turn, src, cap * marginals :].astype(F32)
             for c in range(cap):
-                tops.append(c_in[turn, src, c, marginals:][0:1])
-                asked = req_in[src, c].astype(F32)[0:1]
-                hits.append(asked == eight.astype(F32))
+                tops.append(tile[3 * c : 3 * c + 1] + tile[3 * c + 1 : 3 * c + 2] + tile[3 * c + 2 : 3 * c + 3])
+                hits.append(req_in[src, c : c + 1] == eight.astype(F32))
         best = fold_max(tops, hits)
         totals = [jnp.zeros((marginals, BLOCK), F32) for _ in range(blocks)]
         k = 0
         for src in sources:
             for c in range(cap):
                 scale = jnp.where(hits[k], jnp.exp2(ALPHA * (tops[k] - best)), 0.0)
-                mass = c_in[turn, src, c, 0:marginals]
+                mass = c_in[turn, src, c * marginals : (c + 1) * marginals].astype(F32)
                 for n in range(blocks):
                     totals[n] += scale[n : n + 1] * mass
                 k += 1
@@ -268,7 +277,7 @@
     for d, p in enumerate(far_first):
         src = sub * peers + p
         for c in range(cap):
-            asked = req_in[src, c]
+            asked = asked_block(src, c)
             factor, tile = own_a[0], own_t[0]
             for n in range(1, blocks):
                 hit = asked == n
@@ -378,14 +387,14 @@
             pltpu.VMEM((blocks, TILE, BLOCK), BF16),
             pltpu.VMEM((blocks, marginals, BLOCK), BF16),
             pltpu.VMEM((blocks, depth, BLOCK), BF16),
-            pltpu.VMEM((peers, cap, TILE, BLOCK), BF16),
-            pltpu.VMEM((group, cap, TILE, BLOCK), BF16),
+            pltpu.VMEM((peers, cap, BLOCK), F32),
+            pltpu.VMEM((group, cap, BLOCK), F32),
             pltpu.VMEM((peers, cap, depth, BLOCK), BF16),
             pltpu.VMEM((peers, cap, depth, BLOCK), BF16),
             pltpu.VMEM((2, blocks, BLOCK), F32),
             pltpu.VMEM((2, blocks, BLOCK), F32),
-            pltpu.VMEM((2, peers, cap, marginals + 8, BLOCK), F32),
-            pltpu.VMEM((2, group, cap, marginals + 8, BLOCK), F32),
+            pltpu.VMEM((2, peers, cap * marginals + TILE, BLOCK), BF16),
+            pltpu.VMEM((2, group, cap * marginals + TILE, BLOCK), BF16),
             pltpu.VMEM((blocks, marginals, BLOCK), BF16),
             pltpu.VMEM((blocks, TILE, BLOCK), BF16),
             pltpu.VMEM((peers, cap, 2, TILE, BLOCK), BF16),

time: 38.8 us -> 34.5 us (0.89)
  Pallas kernels: 35.9 us -> 31.5 us
    pallas_call x1, Pallas kernels: 35.9 us -> 31.5 us  [shards(): pl.pallas_call(functools.partial(kernel, peers, cap, blocks, marginals, f...]
where the time goes in v3:
time: 34.5 us; the launch traced here: 34.3 us
  Pallas kernels  31.5 us (91%)
  local copies, waits for them, and re-layouts  2.14 us (6%)
  between operations  0.65 us (2%)
    pallas_call x1, Pallas kernels, shards(): pl.pallas_call(functools.partial(kernel, peers, cap, blocks, marginals, f...  31.5 us
    unnamed x4, local copies, waits for them, and re-layouts  2.14 us

profile of v3, /device:TPU:0, one launch (start us, length us, event | category | flops | bytes accessed | tf_op | source)
XLA Modules:
  0.0 34.3 jit_solution(5778515226969611760)
XLA Ops:
  0.6 31.5 %shard_map.104 = (f32[16,1024]{1,0:T(8,128)}, f32[16,1024]{1,0:T(8,128)}) custom-call(bf16[64,1024]{1,0:T(8,128)(2,1)} %x_hbm.1, bf16[64,1024]{1,0:T(8,128)(2,1)} %y_hbm.1, s32[8,128]{1,0:T(8,128)} %bitcast.4, s32[8,128]{1,0:T(8,128)} %bitcast.5, s32[16,1024]{1,0:T(8,128)} %xw_hbm.1, s32[16,1024]{1,0:T(8,128)} %yw_hbm.1, s32[2,4]{1,0:T(2,128)} %bitcast.6, ...), custom_call_target="tpu_custom_call" | custom-call | tf_op jit(solution)/shard_map/pallas_call | solution.py:366
  32.2 0.0 copy-start
  32.2 1.5 %copy.13 = f32[16,1024]{1,0:T(8,128)} copy(f32[16,1024]{1,0:T(8,128)} %get-tuple-element.4) | data formatting | bytes 131072
  33.7 0.0 copy-done
  33.7 0.6 %copy.14 = f32[16,1024]{1,0:T(8,128)} copy(f32[16,1024]{1,0:T(8,128)S(1)} %copy-done) | data formatting | bytes 131072
Async XLA Ops:
  32.2 1.5 %copy-start = (f32[16,1024]{1,0:T(8,128)S(1)}, f32[16,1024]{1,0:T(8,128)}, u32[]{:S(2)}) copy-start(f32[16,1024]{1,0:T(8,128)} %get-tuple-element.5) | copy-start | bytes 196612

commit v4 on v3

--- a/solution.py
+++ b/solution.py
@@ -46,8 +46,9 @@
 def kernel(
     peers, cap, blocks, marginals, feats,
     x_hbm, y_hbm, xc_hbm, yc_hbm, xw_hbm, yw_hbm, pb_hbm, pr_hbm, pc_hbm,
-    real_out, synth_out,
+    real_hbm, synth_hbm,
     x_ref, y_ref, xc_ref, yc_ref, xw_ref, yw_ref, pb_ref, pr_ref, pc_ref, in_sem,
+    real_out, synth_out, out_sem,
     xf, xt, xu, wr, ys, req_out, req_in, y_out, y_in,
     s1_out, s1_in, c_out, c_in, own_a, own_t, rep_out, rep_in, s2_out, s2_in, bw,
     big_send, big_recv, send, recv, s_send, s_recv,
@@ -335,6 +336,8 @@
         lanes = slice(n * BLOCK, (n + 1) * BLOCK)
         weight = xw_ref[:, lanes].astype(F32) + 0.5
         real_out[:, lanes] = SMOOTH * (jnp.log(weight) - jnp.log(sums[n])) - level[n : n + 1]
+    store_real = pltpu.make_async_copy(real_out, real_hbm, out_sem.at[0])
+    store_real.start()
     best, totals = col_fold(1)
     used = best > 0.5 * SENTINEL
     level = jnp.where(used, best, 0.0)
@@ -343,8 +346,12 @@
         weight = yw_ref[:, lanes].astype(F32) + 0.5
         total = jnp.where(used[n : n + 1], totals[n], 1.0)
         synth_out[:, lanes] = SMOOTH * (jnp.log(weight) - jnp.log(total)) - level[n : n + 1]
+    store_synth = pltpu.make_async_copy(synth_out, synth_hbm, out_sem.at[1])
+    store_synth.start()
     for copy in pending:
         copy.wait_send()
+    store_real.wait()
+    store_synth.wait()
 
 
 def shards(
@@ -361,7 +368,6 @@
     peers, cap = pair_block.shape
     group = 2 * peers
     depth = feats + TILE
-    vmem = pl.BlockSpec(memory_space=pltpu.VMEM)
     hbm = pl.BlockSpec(memory_space=pltpu.HBM)
     real_pot, synth_pot = pl.pallas_call(
         functools.partial(kernel, peers, cap, blocks, marginals, feats),
@@ -370,7 +376,7 @@
             jax.ShapeDtypeStruct((marginals, count), F32),
         ),
         in_specs=[hbm] * 9,
-        out_specs=(vmem, vmem),
+        out_specs=(hbm, hbm),
         scratch_shapes=[
             pltpu.VMEM((feats, count), BF16),
             pltpu.VMEM((feats, count), BF16),
@@ -382,6 +388,9 @@
             pltpu.SMEM((cap, peers), jnp.int32),
             pltpu.SMEM((peers,), jnp.int32),
             pltpu.SemaphoreType.DMA((9,)),
+            pltpu.VMEM((marginals, count), F32),
+            pltpu.VMEM((marginals, count), F32),
+            pltpu.SemaphoreType.DMA((2,)),
             pltpu.VMEM((blocks, feats, BLOCK), BF16),
             pltpu.VMEM((blocks, TILE, BLOCK), BF16),
             pltpu.VMEM((blocks, TILE, BLOCK), BF16),

time: 34.5 us -> 34.4 us (level)
  no operation moved by 1% of the time
where the time goes in v4:
time: 34.4 us; the launch traced here: 34.3 us
  Pallas kernels  31.5 us (92%)
  local copies, waits for them, and re-layouts  2.14 us (6%)
  between operations  0.65 us (2%)
    pallas_call x1, Pallas kernels, shards(): pl.pallas_call(functools.partial(kernel, peers, cap, blocks, marginals, f...  31.5 us
    unnamed x4, local copies, waits for them, and re-layouts  2.14 us

profile of v4, /device:TPU:0, one launch (start us, length us, event | category | flops | bytes accessed | tf_op | source)
XLA Modules:
  0.0 34.3 jit_solution(11027126259033889093)
XLA Ops:
  0.6 31.5 %shard_map.104 = (f32[16,1024]{1,0:T(8,128)}, f32[16,1024]{1,0:T(8,128)}) custom-call(bf16[64,1024]{1,0:T(8,128)(2,1)} %x_hbm.1, bf16[64,1024]{1,0:T(8,128)(2,1)} %y_hbm.1, s32[8,128]{1,0:T(8,128)} %bitcast.4, s32[8,128]{1,0:T(8,128)} %bitcast.5, s32[16,1024]{1,0:T(8,128)} %xw_hbm.1, s32[16,1024]{1,0:T(8,128)} %yw_hbm.1, s32[2,4]{1,0:T(2,128)} %bitcast.6, ...), custom_call_target="tpu_custom_call" | custom-call | tf_op jit(solution)/shard_map/pallas_call | solution.py:372
  32.1 0.0 copy-start
  32.1 1.5 %copy.13 = f32[16,1024]{1,0:T(8,128)} copy(f32[16,1024]{1,0:T(8,128)} %get-tuple-element.4) | data formatting | bytes 131072
  33.6 0.0 copy-done
  33.6 0.6 %copy.14 = f32[16,1024]{1,0:T(8,128)} copy(f32[16,1024]{1,0:T(8,128)S(1)} %copy-done) | data formatting | bytes 131072
Async XLA Ops:
  32.1 1.5 %copy-start = (f32[16,1024]{1,0:T(8,128)S(1)}, f32[16,1024]{1,0:T(8,128)}, u32[]{:S(2)}) copy-start(f32[16,1024]{1,0:T(8,128)} %get-tuple-element.5) | copy-start | bytes 196612
